TPU v7x, 512 devices: a whole 4x8x8 slice. The times are simulated.
512 devices in a mesh: expert: 64 (over x, z, core), replica: 8 (over y).
Axes of the slice: x: 4, y: 8, z: 8, core: 2. Of those that a mesh axis runs over, the one named last changes fastest.
Arguments:
- tokens: bfloat16 [768, 3584], P('expert', 'replica'), may hold values from -6 to 6
- expert_ids: int32 [768, 8], P('expert'), may hold values from 0 to 31, all different within a row; in each aligned block of 12 rows (0 to 11, 12 to 23, ...) at most 4 rows name the same one
- gate_values: float32 [768, 8], P('expert'), may hold values from 0.1 to 0.6
- gate_weight: bfloat16 [64, 512, 3584], P('expert', 'replica'), may hold values from -0.09375 to 0.09375
- up_weight: bfloat16 [64, 512, 3584], P('expert', 'replica'), may hold values from -0.09375 to 0.09375
- down_weight: bfloat16 [64, 512, 3584], P('expert', None, 'replica'), may hold values from -0.1875 to 0.1875
- out_grad: bfloat16 [768, 3584], P('expert', 'replica'), may hold values from -1.5 to 1.5
Outputs:
- moe_out: bfloat16 [768, 3584], P('expert', 'replica')
- token_grad: bfloat16 [768, 3584], P('expert', 'replica')
- gate_grad: bfloat16 [64, 512, 3584], P('expert', 'replica')
- up_grad: bfloat16 [64, 512, 3584], P('expert', 'replica')
- down_grad: bfloat16 [64, 512, 3584], P('expert', None, 'replica')
Inputs may be any that keep to these rules, and one draw needn't show every extreme that they name: `expert_ids`: each row names 8 different experts. Among the 12 rows of one index of expert, no expert is named by more than 4 rows, a bound that some block reaches.
All inputs are finite; a program needn't handle non-finite values.
Results may differ from a plain program's by a relative error of at most 0.0075.
Values may be sent and summed in bfloat16 or wider, within the bound.
A program may use at most 64 MiB of HBM per device.

v0:
```python
import jax
import jax.numpy as jnp
from jax import lax
from jax.sharding import PartitionSpec as P


def partner_2(block, axis, distance):
    count = lax.axis_size(axis)
    route = []
    for low in range(count):
        high = low | 1 << distance
        if high != low and high < count:
            route += [(low, high), (high, low)]
    return lax.ppermute(block, axis, route)


def pair_join(parity_bit, own_part, peer_part, stack_axis):
    first_part = jnp.where(parity_bit == 0, own_part, peer_part)
    second_part = jnp.where(parity_bit == 0, peer_part, own_part)
    return jnp.stack([first_part, second_part], axis=stack_axis)


def pick_half(parity_bit, stacked, stack_axis):
    lower = jnp.take(stacked, 0, axis=stack_axis)
    higher = jnp.take(stacked, 1, axis=stack_axis)
    return (jnp.where(parity_bit == 0, lower, higher), jnp.where(parity_bit == 0, higher, lower))


def per_device(tokens, expert_ids, gate_values, gate_weight, up_weight, down_weight, out_grad):
    experts_axis = lax.axis_size("expert")
    tok_rows, slice_width = tokens.shape
    top_count = expert_ids.shape[1]
    expert_count = experts_axis // 2
    most_rows = min(tok_rows, 4 * tok_rows * top_count // (3 * expert_count))
    capacity = (most_rows + 1) // 2
    pair_count = tok_rows * top_count
    slot_count = experts_axis * capacity
    flat_ids = expert_ids.reshape(pair_count)
    onehot = (flat_ids[:, None] == jnp.arange(expert_count, dtype=jnp.int32)[None, :]).astype(
        jnp.int32
    )
    rank_in = jnp.sum((jnp.cumsum(onehot, axis=0) - onehot) * onehot, axis=1)
    upper_copy = (rank_in >= capacity).astype(jnp.int32)
    target = (2 * flat_ids + upper_copy) * capacity + rank_in - upper_copy * capacity
    slot_match = target[None, :] == jnp.arange(slot_count, dtype=jnp.int32)[:, None]
    filled = jnp.any(slot_match, axis=1)
    source_pair = jnp.sum(
        jnp.where(slot_match, jnp.arange(pair_count, dtype=jnp.int32)[None, :], 0), axis=1
    )
    source_token = source_pair // top_count
    flat_gates = gate_values.reshape(pair_count)
    send_rows = jnp.where(filled[:, None], tokens[source_token], jnp.zeros((), tokens.dtype))
    scaled = flat_gates[source_pair][:, None] * out_grad[source_token].astype(jnp.float32)
    send_grads = jnp.where(filled[:, None], scaled, 0.0).astype(jnp.bfloat16)
    got_rows, got_grads = (
        lax.all_to_all(
            send_rows.reshape(experts_axis, capacity, slice_width),
            "expert",
            split_axis=0,
            concat_axis=0,
            tiled=True,
        ),
        lax.all_to_all(
            send_grads.reshape(experts_axis, capacity, slice_width),
            "expert",
            split_axis=0,
            concat_axis=0,
            tiled=True,
        ),
    )
    rows_part = got_rows.reshape(slot_count, slice_width)
    grads_part = got_grads.reshape(slot_count, slice_width)
    parity_bit = lax.axis_index("expert") % 2
    own_pieces = (gate_weight[0], up_weight[0], down_weight[0])
    partner = partner_2((own_pieces[0], own_pieces[1], own_pieces[2]), "expert", 0)
    w_gate = pair_join(parity_bit, own_pieces[0], partner[0], 0)
    w_up = pair_join(parity_bit, own_pieces[1], partner[1], 0)
    w_down = pair_join(parity_bit, own_pieces[2], partner[2], 0)
    _, quarter, model_width = w_gate.shape
    full_rows = lax.all_gather(rows_part, "replica", axis=1, tiled=True)
    contract = (((1,), (1,)), ((), ()))
    pre_gate = lax.dot_general(
        full_rows,
        w_gate.reshape(2 * quarter, model_width),
        contract,
        preferred_element_type=jnp.float32,
    ).reshape(slot_count, 2, quarter)
    pre_up = lax.dot_general(
        full_rows,
        w_up.reshape(2 * quarter, model_width),
        contract,
        preferred_element_type=jnp.float32,
    ).reshape(slot_count, 2, quarter)
    sigma = jax.nn.sigmoid(pre_gate)
    activated = pre_gate * sigma
    slope_term = sigma * (1.0 + pre_gate * (1.0 - sigma))
    hidden = (activated * pre_up).astype(jnp.bfloat16)
    all_hidden = lax.all_gather(hidden, "replica", axis=2, tiled=True).reshape(slot_count, -1)
    down_full = w_down.reshape(-1, slice_width)
    expert_out = jnp.dot(all_hidden, down_full, preferred_element_type=jnp.float32).astype(
        jnp.bfloat16
    )
    returned = lax.all_to_all(
        expert_out.reshape(experts_axis, capacity, slice_width),
        "expert",
        split_axis=0,
        concat_axis=0,
        tiled=True,
    ).reshape(slot_count, slice_width)
    picked = returned[target].astype(jnp.float32).reshape(tok_rows, top_count, slice_width)
    moe_out = jnp.sum(picked * gate_values[:, :, None], axis=1).astype(jnp.bfloat16)
    down_local = lax.dot_general(
        all_hidden, grads_part, (((0,), (0,)), ((), ())), preferred_element_type=jnp.float32
    )
    full_grads = lax.all_gather(grads_part, "replica", axis=1, tiled=True)
    down_rows = lax.all_to_all(w_down, "replica", split_axis=1, concat_axis=2, tiled=True)
    hidden_grad = jnp.einsum(
        "sd,hqd->shq", full_grads, down_rows, preferred_element_type=jnp.float32
    )
    gate_act = (hidden_grad * pre_up * slope_term).astype(jnp.bfloat16)
    up_act = (hidden_grad * activated).astype(jnp.bfloat16)
    gate_local = jnp.einsum("sd,shq->hqd", full_rows, gate_act, preferred_element_type=jnp.float32)
    up_local = jnp.einsum("sd,shq->hqd", full_rows, up_act, preferred_element_type=jnp.float32)
    all_gate_act, all_up_act = (
        lax.all_gather(gate_act, "replica", axis=2, tiled=True),
        lax.all_gather(up_act, "replica", axis=2, tiled=True),
    )
    rows_gate, rows_up = (
        lax.all_to_all(w_gate, "replica", split_axis=2, concat_axis=1, tiled=True),
        lax.all_to_all(w_up, "replica", split_axis=2, concat_axis=1, tiled=True),
    )
    input_rows = jnp.einsum(
        "shf,hfd->sd", all_gate_act, rows_gate, preferred_element_type=jnp.float32
    )
    input_rows = input_rows + jnp.einsum(
        "shf,hfd->sd", all_up_act, rows_up, preferred_element_type=jnp.float32
    )
    grads_back = lax.all_to_all(
        input_rows.astype(jnp.bfloat16).reshape(experts_axis, capacity, slice_width),
        "expert",
        split_axis=0,
        concat_axis=0,
        tiled=True,
    ).reshape(slot_count, slice_width)
    token_grad = jnp.sum(
        grads_back[target].astype(jnp.float32).reshape(tok_rows, top_count, slice_width), axis=1
    ).astype(jnp.bfloat16)
    keep_gate, give_gate = pick_half(parity_bit, gate_local, 0)
    keep_up, give_up = pick_half(parity_bit, up_local, 0)
    keep_down, give_down = pick_half(parity_bit, down_local.reshape(2, -1, slice_width), 0)
    received = (
        partner_2(give_gate.astype(jnp.bfloat16), "expert", 0).astype(give_gate.dtype),
        partner_2(give_up.astype(jnp.bfloat16), "expert", 0).astype(give_up.dtype),
        partner_2(give_down.astype(jnp.bfloat16), "expert", 0).astype(give_down.dtype),
    )
    gate_grad = (keep_gate + received[0]).astype(jnp.bfloat16)[None]
    up_grad = (keep_up + received[1]).astype(jnp.bfloat16)[None]
    down_grad = (keep_down + received[2]).astype(jnp.bfloat16)[None]
    return (moe_out, token_grad, gate_grad, up_grad, down_grad)


def solution(mesh):
    placed = (
        P("expert", "replica"),
        P("expert", None),
        P("expert", None),
        P("expert", "replica", None),
        P("expert", "replica", None),
        P("expert", None, "replica"),
        P("expert", "replica"),
    )
    return jax.shard_map(
        per_device,
        mesh=mesh,
        in_specs=placed,
        out_specs=(
            P("expert", "replica"),
            P("expert", "replica"),
            P("expert", "replica", None),
            P("expert", "replica", None),
            P("expert", None, "replica"),
        ),
        check_vma=False,
    )
```

profile of v0, /device:TPU:1, one launch (start us, length us, event | category | flops | bytes accessed | tf_op | source)
XLA Modules:
  0.0 322.7 jit_solution(3056633494185465903)
XLA Ops:
  0.7 8.9 %collective-permute-start.2 = (bf16[512,448]{0,1:T(8,128)(2,1)}, bf16[512,448]{0,1:T(8,128)(2,1)S(1)}, u32[]{:S(2)}, u32[]{:S(2)}) collective-permute-start(bf16[512,448]{0,1:T(8,128)(2,1)} %bitcast.169), channel_id=1, source_target_pairs={{0,8},{8,0},{16,24},{24,16},{32,40},{40,32},{48,56},{56,48},{64,72... | collective-permute-start | bytes 1376264 | tf_op jit(solution)/shard_map/ppermute | solution.py:14
  15.9 8.1 %all-to-all-start.2 = ((bf16[64,2,448]{2,1,0:T(2,128)(2,1)}), bf16[64,2,448]{2,1,0:T(2,128)(2,1)S(1)}, u32[]{:S(2)}, u32[]{:S(2)}) async-start(bf16[64,2,448]{2,1,0:T(2,128)(2,1)} %select_convert_fusion.3), calls=%async_computation.2 | async-start | bytes 262144 | tf_op jit(solution)/shard_map/all_to_all | solution.py:63
  24.0 2.4 collective-permute-start.1
  30.4 4.0 %all-to-all-done.2 = bf16[64,2,448]{2,1,0:T(2,128)(2,1)S(1)} async-done(((bf16[64,2,448]{2,1,0:T(2,128)(2,1)}), bf16[64,2,448]{2,1,0:T(2,128)(2,1)S(1)}, u32[]{:S(2)}, u32[]{:S(2)}) %all-to-all-start.2) | async-done | bytes 114720 | tf_op jit(solution)/shard_map/all_to_all | solution.py:63
  34.4 6.3 %all-to-all-start = ((bf16[64,2,448]{2,1,0:T(2,128)(2,1)}), bf16[64,2,448]{2,1,0:T(2,128)(2,1)S(1)}, u32[]{:S(2)}, u32[]{:S(2)}) async-start(bf16[64,2,448]{2,1,0:T(2,128)(2,1)} %broadcast_select_fusion), calls=%async_computation | async-start | bytes 262144 | tf_op jit(solution)/shard_map/all_to_all | solution.py:56
  41.6 9.5 %all-to-all-done = bf16[64,2,448]{2,1,0:T(2,128)(2,1)S(1)} async-done(((bf16[64,2,448]{2,1,0:T(2,128)(2,1)}), bf16[64,2,448]{2,1,0:T(2,128)(2,1)S(1)}, u32[]{:S(2)}, u32[]{:S(2)}) %all-to-all-start) | async-done | bytes 114720 | tf_op jit(solution)/shard_map/all_to_all | solution.py:56
  51.3 24.1 %all_gather.17 = bf16[128,3584]{0,1:T(8,128)(2,1)} all-gather(bf16[128,448]{0,1:T(8,128)(2,1)S(1)} %copy.62), channel_id=1, replica_groups=mesh['expert'=64,'replica'=8] {'replica'}, dimensions={1}, use_global_device_ids=true | all-gather | bytes 1032192 | tf_op jit(solution)/shard_map/all_gather | solution.py:115
  77.7 6.0 %all-to-all-start.3 = ((bf16[2,512,448]{2,0,1:T(2,128)(2,1)}), bf16[2,512,448]{2,0,1:T(2,128)(2,1)}, u32[]{:S(2)}, u32[]{:S(2)}) async-start(bf16[2,512,448]{2,0,1:T(2,128)(2,1)} %copy.63), calls=%async_computation.3 | async-start | bytes 2097152 | tf_op jit(solution)/shard_map/all_to_all | solution.py:116
  83.7 41.3 %all_gather.15 = bf16[128,3584]{0,1:T(8,128)(2,1)S(1)} all-gather(bf16[128,448]{0,1:T(8,128)(2,1)S(1)} %copy.57), channel_id=1, replica_groups=mesh['expert'=64,'replica'=8] {'replica'}, dimensions={1}, use_global_device_ids=true | all-gather | bytes 1032192 | tf_op jit(solution)/shard_map/all_gather | solution.py:80
  128.0 4.3 %copy.69 = bf16[2,64,3584]{1,0,2:T(2,128)(2,1)S(1)} copy(bf16[2,64,3584]{2,1,0:T(8,128)(2,1)} %pad_maximum_fusion.2) | data formatting | bytes 1835008 | tf_op jit(solution)/shard_map/stack | solution.py:20
  134.4 4.2 %all-to-all-start.5 = ((bf16[8,2,28672]{2,1,0:T(2,128)(2,1)}), bf16[8,2,28672]{2,1,0:T(2,128)(2,1)}, u32[]{:S(2)}, u32[]{:S(2)}) async-start(bf16[8,2,28672]{2,1,0:T(2,128)(2,1)} %reshape.363), calls=%async_computation.5 | async-start | bytes 1835008 | tf_op jit(solution)/shard_map/all_to_all | solution.py:130
  141.9 4.3 %copy.66 = bf16[2,64,3584]{1,0,2:T(2,128)(2,1)S(1)} copy(bf16[2,64,3584]{2,1,0:T(8,128)(2,1)} %pad_maximum_fusion.1) | data formatting | bytes 1835008 | tf_op jit(solution)/shard_map/stack | solution.py:20
  154.5 6.7 %all-to-all-start.4 = ((bf16[8,2,28672]{2,1,0:T(2,128)(2,1)}), bf16[8,2,28672]{2,1,0:T(2,128)(2,1)}, u32[]{:S(2)}, u32[]{:S(2)}) async-start(bf16[8,2,28672]{2,1,0:T(2,128)(2,1)} %reshape.365), calls=%async_computation.4 | async-start | bytes 1835008 | tf_op jit(solution)/shard_map/all_to_all | solution.py:129
  162.8 30.9 %all_gather.16 = bf16[128,2,512]{0,2,1:T(8,128)(2,1)S(1)} all-gather(bf16[128,2,64]{0,2,1:T(8,128)(2,1)S(1)} %get-tuple-element.61), channel_id=1, replica_groups=mesh['expert'=64,'replica'=8] {'replica'}, dimensions={2}, use_global_device_ids=true | all-gather | bytes 294912 | tf_op jit(solution)/shard_map/all_gather | solution.py:98
  195.1 4.5 %reshape.364 = bf16[3584,2,64]{2,1,0:T(2,128)(2,1)S(1)} reshape(bf16[8,2,28672]{2,1,0:T(2,128)(2,1)} %all-to-all-done.5) | data formatting | bytes 1835008
  199.6 3.5 %copy.70 = bf16[2,64,8,448]{3,1,2,0:T(8,128)(2,1)} copy(bf16[2,64,8,448]{1,0,3,2:T(2,128)(2,1)S(1)} %bitcast.164) | data formatting | bytes 1835008 | tf_op jit(solution)/shard_map/all_to_all | solution.py:130
  203.1 18.4 %all_gather.19 = bf16[128,2,512]{0,2,1:T(8,128)(2,1)S(1)} all-gather(bf16[128,2,64]{0,2,1:T(8,128)(2,1)S(1)} %get-tuple-element.60), channel_id=1, replica_groups=mesh['expert'=64,'replica'=8] {'replica'}, dimensions={2}, use_global_device_ids=true | all-gather | bytes 294912 | tf_op jit(solution)/shard_map/all_gather | solution.py:126
  221.5 18.8 %all_gather.18 = bf16[128,2,512]{0,2,1:T(8,128)(2,1)S(1)} all-gather(bf16[128,2,64]{0,2,1:T(8,128)(2,1)S(1)} %get-tuple-element.59), channel_id=1, replica_groups=mesh['expert'=64,'replica'=8] {'replica'}, dimensions={2}, use_global_device_ids=true | all-gather | bytes 294912 | tf_op jit(solution)/shard_map/all_gather | solution.py:125
  242.3 27.9 %all-to-all-start.1 = ((bf16[64,2,448]{2,1,0:T(2,128)(2,1)}), bf16[64,2,448]{2,1,0:T(2,128)(2,1)S(1)}, u32[]{:S(2)}, u32[]{:S(2)}) async-start(bf16[64,2,448]{2,1,0:T(2,128)(2,1)} %reshape.212), calls=%async_computation.1 | async-start | bytes 262144 | tf_op jit(solution)/shard_map/all_to_all | solution.py:103
  270.2 5.3 %reshape.366 = bf16[3584,2,64]{2,1,0:T(2,128)(2,1)} reshape(bf16[8,2,28672]{2,1,0:T(2,128)(2,1)} %all-to-all-done.4) | data formatting | bytes 1835008
  275.5 5.8 %copy.67 = bf16[2,64,8,448]{3,1,2,0:T(8,128)(2,1)} copy(bf16[2,64,8,448]{1,0,3,2:T(2,128)(2,1)} %bitcast.165) | data formatting | bytes 1835008 | tf_op jit(solution)/shard_map/all_to_all | solution.py:129
  293.0 10.3 %all-to-all-start.6 = ((bf16[64,2,448]{2,1,0:T(2,128)(2,1)}), bf16[64,2,448]{2,1,0:T(2,128)(2,1)S(1)}, u32[]{:S(2)}, u32[]{:S(2)}) async-start(bf16[64,2,448]{2,1,0:T(2,128)(2,1)} %reshape.216), calls=%async_computation.6 | async-start | bytes 262144 | tf_op jit(solution)/shard_map/all_to_all | solution.py:138
  308.2 5.4 %all-to-all-done.6 = bf16[64,2,448]{2,1,0:T(2,128)(2,1)S(1)} async-done(((bf16[64,2,448]{2,1,0:T(2,128)(2,1)}), bf16[64,2,448]{2,1,0:T(2,128)(2,1)S(1)}, u32[]{:S(2)}, u32[]{:S(2)}) %all-to-all-start.6) | async-done | bytes 114720 | tf_op jit(solution)/shard_map/all_to_all | solution.py:138
  316.1 2.5 fusion.13
  (124 shorter events, 58.2 us)
Async XLA Ops:
  0.6 10.5 %copy-start = (bf16[12,448]{1,0:T(8,128)(2,1)S(1)}, bf16[12,448]{1,0:T(8,128)(2,1)}, u32[]{:S(2)}) copy-start(bf16[12,448]{1,0:T(8,128)(2,1)} %param.21) | copy-start | bytes 32260
  0.6 27.7 %copy-start.20 = (s32[12,8]{0,1:T(8,128)S(1)}, s32[12,8]{0,1:T(8,128)}, u32[]{:S(2)}) copy-start(s32[12,8]{0,1:T(8,128)} %param.16) | copy-start | bytes 1156
  0.7 23.4 %copy-start.17 = (bf16[1,64,3584]{2,1,0:T(8,128)(2,1)S(1)}, bf16[1,64,3584]{2,1,0:T(8,128)(2,1)}, u32[]{:S(2)}) copy-start(bf16[1,64,3584]{2,1,0:T(8,128)(2,1)} %param.19) | copy-start | bytes 1376260
  0.7 27.7 %copy-start.1 = (bf16[12,448]{1,0:T(8,128)(2,1)S(1)}, bf16[12,448]{1,0:T(8,128)(2,1)}, u32[]{:S(2)}) copy-start(bf16[12,448]{1,0:T(8,128)(2,1)} %param.15) | copy-start | bytes 32260
  0.7 74.7 %collective-permute-start.2 = (bf16[512,448]{0,1:T(8,128)(2,1)}, bf16[512,448]{0,1:T(8,128)(2,1)S(1)}, u32[]{:S(2)}, u32[]{:S(2)}) collective-permute-start(bf16[512,448]{0,1:T(8,128)(2,1)} %bitcast.169), channel_id=1, source_target_pairs={{0,8},{8,0},{16,24},{24,16},{32,40},{40,32},{48,56},{56,48},{64,72... | collective-permute-start | bytes 1376264 | tf_op jit(solution)/shard_map/ppermute | solution.py:14
  15.9 18.4 %all-to-all-start.2 = ((bf16[64,2,448]{2,1,0:T(2,128)(2,1)}), bf16[64,2,448]{2,1,0:T(2,128)(2,1)S(1)}, u32[]{:S(2)}, u32[]{:S(2)}) async-start(bf16[64,2,448]{2,1,0:T(2,128)(2,1)} %select_convert_fusion.3), calls=%async_computation.2 | async-start | bytes 262144 | tf_op jit(solution)/shard_map/all_to_all | solution.py:63
  24.0 101.0 %collective-permute-start.1 = (bf16[64,3584]{1,0:T(8,128)(2,1)S(1)}, bf16[64,3584]{1,0:T(8,128)(2,1)}, u32[]{:S(2)}, u32[]{:S(2)}) collective-permute-start(bf16[64,3584]{1,0:T(8,128)(2,1)S(1)} %bitcast.170), channel_id=1, source_target_pairs={{0,8},{8,0},{16,24},{24,16},{32,40},{40,32},{48,56},{56,48},{64,72... | collective-permute-start | bytes 1376264 | tf_op jit(solution)/shard_map/ppermute | solution.py:14
  26.4 112.3 %collective-permute-start = (bf16[64,3584]{1,0:T(8,128)(2,1)}, bf16[64,3584]{1,0:T(8,128)(2,1)}, u32[]{:S(2)}, u32[]{:S(2)}) collective-permute-start(bf16[64,3584]{1,0:T(8,128)(2,1)} %bitcast.3), channel_id=1, source_target_pairs={{0,8},{8,0},{16,24},{24,16},{32,40},{40,32},{48,56},{56,48},{64,72... | collective-permute-start | bytes 1376264 | tf_op jit(solution)/shard_map/ppermute | solution.py:14
  28.4 47.0 %copy-start.16 = (bf16[1,512,448]{1,2,0:T(8,128)(2,1)S(1)}, bf16[1,512,448]{1,2,0:T(8,128)(2,1)}, u32[]{:S(2)}) copy-start(bf16[1,512,448]{1,2,0:T(8,128)(2,1)} %param.20) | copy-start | bytes 1376260
  34.4 16.7 %all-to-all-start = ((bf16[64,2,448]{2,1,0:T(2,128)(2,1)}), bf16[64,2,448]{2,1,0:T(2,128)(2,1)S(1)}, u32[]{:S(2)}, u32[]{:S(2)}) async-start(bf16[64,2,448]{2,1,0:T(2,128)(2,1)} %broadcast_select_fusion), calls=%async_computation | async-start | bytes 262144 | tf_op jit(solution)/shard_map/all_to_all | solution.py:56
  77.7 56.7 %all-to-all-start.3 = ((bf16[2,512,448]{2,0,1:T(2,128)(2,1)}), bf16[2,512,448]{2,0,1:T(2,128)(2,1)}, u32[]{:S(2)}, u32[]{:S(2)}) async-start(bf16[2,512,448]{2,0,1:T(2,128)(2,1)} %copy.63), calls=%async_computation.3 | async-start | bytes 2097152 | tf_op jit(solution)/shard_map/all_to_all | solution.py:116
  134.4 20.1 %all-to-all-start.5 = ((bf16[8,2,28672]{2,1,0:T(2,128)(2,1)}), bf16[8,2,28672]{2,1,0:T(2,128)(2,1)}, u32[]{:S(2)}, u32[]{:S(2)}) async-start(bf16[8,2,28672]{2,1,0:T(2,128)(2,1)} %reshape.363), calls=%async_computation.5 | async-start | bytes 1835008 | tf_op jit(solution)/shard_map/all_to_all | solution.py:130
  152.4 8.8 %copy-start.4 = (bf16[128,3584]{0,1:T(8,128)(2,1)S(1)}, bf16[128,3584]{0,1:T(8,128)(2,1)}, u32[]{:S(2)}) copy-start(bf16[128,3584]{0,1:T(8,128)(2,1)} %all_gather.17) | copy-start | bytes 2752516
  154.5 6.7 %copy-start.5 = (bf16[2,64,3584]{2,1,0:T(8,128)(2,1)S(1)}, bf16[2,64,3584]{2,1,0:T(8,128)(2,1)}, u32[]{:S(2)}) copy-start(bf16[2,64,3584]{2,1,0:T(8,128)(2,1)} %all_to_all.57) | copy-start | bytes 2752516
  154.5 7.1 %copy-start.21 = (f32[128,2,64]{0,2,1:T(8,128)S(1)}, f32[128,2,64]{0,2,1:T(8,128)}, u32[]{:S(2)}) copy-start(f32[128,2,64]{0,2,1:T(8,128)} %fusion.9) | copy-start | bytes 196612
  154.5 87.8 %all-to-all-start.4 = ((bf16[8,2,28672]{2,1,0:T(2,128)(2,1)}), bf16[8,2,28672]{2,1,0:T(2,128)(2,1)}, u32[]{:S(2)}, u32[]{:S(2)}) async-start(bf16[8,2,28672]{2,1,0:T(2,128)(2,1)} %reshape.365), calls=%async_computation.4 | async-start | bytes 1835008 | tf_op jit(solution)/shard_map/all_to_all | solution.py:129
  162.3 31.3 %copy-start.7 = (bf16[1,512,448]{1,2,0:T(8,128)(2,1)S(1)}, bf16[1,512,448]{1,2,0:T(8,128)(2,1)}, u32[]{:S(2)}) copy-start(bf16[1,512,448]{1,2,0:T(8,128)(2,1)} %copy-done.6) | copy-start | bytes 1376260
  242.3 50.6 %all-to-all-start.1 = ((bf16[64,2,448]{2,1,0:T(2,128)(2,1)}), bf16[64,2,448]{2,1,0:T(2,128)(2,1)S(1)}, u32[]{:S(2)}, u32[]{:S(2)}) async-start(bf16[64,2,448]{2,1,0:T(2,128)(2,1)} %reshape.212), calls=%async_computation.1 | async-start | bytes 262144 | tf_op jit(solution)/shard_map/all_to_all | solution.py:103
  283.7 7.6 %copy-start.15 = (bf16[128,2,512]{0,2,1:T(8,128)(2,1)S(1)}, bf16[128,2,512]{0,2,1:T(8,128)(2,1)}, u32[]{:S(2)}) copy-start(bf16[128,2,512]{0,2,1:T(8,128)(2,1)} %copy-done.14) | copy-start | bytes 786436
  286.9 29.2 %collective-permute-start.3 = (bf16[64,3584]{1,0:T(8,128)(2,1)}, bf16[64,3584]{1,0:T(8,128)(2,1)}, u32[]{:S(2)}, u32[]{:S(2)}) collective-permute-start(bf16[64,3584]{1,0:T(8,128)(2,1)} %select_convert_fusion.2), channel_id=1, source_target_pairs={{0,8},{8,0},{16,24},{24,16},{32,40},{40,32},{48,56},{56,48},{64,72... | collective-permute-start | bytes 1376264 | tf_op jit(solution)/shard_map/ppermute | solution.py:14
  289.3 29.2 %collective-permute-start.4 = (bf16[64,3584]{1,0:T(8,128)(2,1)S(1)}, bf16[64,3584]{1,0:T(8,128)(2,1)}, u32[]{:S(2)}, u32[]{:S(2)}) collective-permute-start(bf16[64,3584]{1,0:T(8,128)(2,1)S(1)} %select_convert_fusion.1), channel_id=1, source_target_pairs={{0,8},{8,0},{16,24},{24,16},{32,40},{40,32},{48,56},{56,48},{64,72... | collective-permute-start | bytes 1376264 | tf_op jit(solution)/shard_map/ppermute | solution.py:14
  293.0 20.7 %all-to-all-start.6 = ((bf16[64,2,448]{2,1,0:T(2,128)(2,1)}), bf16[64,2,448]{2,1,0:T(2,128)(2,1)S(1)}, u32[]{:S(2)}, u32[]{:S(2)}) async-start(bf16[64,2,448]{2,1,0:T(2,128)(2,1)} %reshape.216), calls=%async_computation.6 | async-start | bytes 262144 | tf_op jit(solution)/shard_map/all_to_all | solution.py:138
  303.3 12.1 %copy-start.19 = (f32[12,8]{1,0:T(8,128)S(1)}, f32[12,8]{1,0:T(8,128)}, u32[]{:S(2)}) copy-start(f32[12,8]{1,0:T(8,128)} %copy-done.18) | copy-start | bytes 1156
  304.8 15.7 %collective-permute-start.5 = (bf16[512,448]{0,1:T(8,128)(2,1)S(1)}, bf16[512,448]{0,1:T(8,128)(2,1)}, u32[]{:S(2)}, u32[]{:S(2)}) collective-permute-start(bf16[512,448]{0,1:T(8,128)(2,1)S(1)} %select_convert_fusion), channel_id=1, source_target_pairs={{0,8},{8,0},{16,24},{24,16},{32,40},{40,32},{48,56},{56,48},{64,72... | collective-permute-start | bytes 1376264 | tf_op jit(solution)/shard_map/ppermute | solution.py:14
  (11 other events, 13.0 us)
where the time goes:
time: 324 us; the launch traced here: 323 us
  blocking collectives  133 us (41%)
  starting transfers between devices  89.4 us (28%)
  local copies, waits for them, and re-layouts  50.9 us (16%)
  other arithmetic  19.4 us (6%)
  waiting for transfers between devices  18.9 us (6%)
  matrix products  9.43 us (3%)
    all_gather x1, blocking collectives, per_device(): full_rows = lax.all_gather(rows_part, 'replica', axis=1, tiled=True)  41.3 us
    all_gather x1, blocking collectives, per_device(): lax.all_gather(hidden, 'replica', axis=2, tiled=True)  30.9 us
    all_to_all x1, starting transfers between devices, per_device(): lax.all_to_all(expert_out.reshape(experts_axis, capacity, slice_width), '...  27.9 us
    all_gather x1, blocking collectives, per_device(): full_grads = lax.all_gather(grads_part, 'replica', axis=1, tiled=True)  24.1 us
    ppermute x6, starting transfers between devices, partner_2(): return lax.ppermute(block, axis, route)  19.9 us
    unnamed x50, local copies, waits for them, and re-layouts  18.8 us
    all_gather x1, blocking collectives, per_device(): lax.all_gather(gate_act, 'replica', axis=2, tiled=True)  18.8 us
    all_gather x1, blocking collectives, per_device(): lax.all_gather(up_act, 'replica', axis=2, tiled=True)  18.4 us
  transfers between devices with their start and end apart: 13, of which 3 were waited for; matrix products, arithmetic and copies ran while one was open for 22% of the time, Pallas kernels for 0%

commit v1 on v0

--- a/solution.py
+++ b/solution.py
@@ -122,7 +122,10 @@
     gate_local = jnp.einsum("sd,shq->hqd", full_rows, gate_act, preferred_element_type=jnp.float32)
     up_local = jnp.einsum("sd,shq->hqd", full_rows, up_act, preferred_element_type=jnp.float32)
     all_gate_act, all_up_act = (
-        lax.all_gather(gate_act, "replica", axis=2, tiled=True),
+        jnp.concatenate(
+            lax.all_to_all(jnp.stack([gate_act] * lax.axis_size("replica")), "replica", 0, 0),
+            axis=2,
+        ),
         lax.all_gather(up_act, "replica", axis=2, tiled=True),
     )
     rows_gate, rows_up = (

time: 324 us -> 314 us (0.969)
  blocking collectives: 133 us -> 117 us
  waiting for transfers between devices: 18.9 us -> 26.4 us
  starting transfers between devices: 89.4 us -> 82.2 us
  local copies, waits for them, and re-layouts: 50.9 us -> 56.2 us
    all_to_all x1, starting transfers between devices: 27.9 us -> 4.89 us  [per_device(): lax.all_to_all(expert_out.reshape(experts_axis, capacity, slice_width), '...]
    all_gather x1 -> x0, blocking collectives: 18.8 us -> none  [per_device(): lax.all_gather(gate_act, 'replica', axis=2, tiled=True)]
    ppermute x6, starting transfers between devices: 19.9 us -> 30.7 us  [partner_2(): return lax.ppermute(block, axis, route)]
    all_to_all x1, waiting for transfers between devices: 0.01 us -> 8.68 us  [per_device(): lax.all_to_all(expert_out.reshape(experts_axis, capacity, slice_width), '...]
    all_to_all x0 -> x1, starting transfers between devices: none -> 4.91 us  [per_device(): lax.all_to_all(jnp.stack([gate_act] * lax.axis_size('replica')), 'replica...]
    unnamed x50 -> x46, local copies, waits for them, and re-layouts: 18.8 us -> 20.7 us
  transfers between devices with their start and end apart: 13 -> 14, of which waited for: 3 -> 4; matrix products, arithmetic and copies ran while one was open for 22% -> 25% of each run, Pallas kernels for 0% -> 0%
where the time goes in v1:
time: 314 us; the launch traced here: 312 us
  blocking collectives  117 us (37%)
  starting transfers between devices  82.2 us (26%)
  local copies, waits for them, and re-layouts  56.2 us (18%)
  waiting for transfers between devices  26.4 us (8%)
  other arithmetic  20.1 us (6%)
  matrix products  8.77 us (3%)
    all_gather x1, blocking collectives, per_device(): full_rows = lax.all_gather(rows_part, 'replica', axis=1, tiled=True)  41.3 us
    all_gather x1, blocking collectives, per_device(): lax.all_gather(hidden, 'replica', axis=2, tiled=True)  31.6 us
    ppermute x6, starting transfers between devices, partner_2(): return lax.ppermute(block, axis, route)  30.7 us
    all_gather x1, blocking collectives, per_device(): full_grads = lax.all_gather(grads_part, 'replica', axis=1, tiled=True)  24.1 us
    unnamed x46, local copies, waits for them, and re-layouts  20.7 us
    all_gather x1, blocking collectives, per_device(): lax.all_gather(up_act, 'replica', axis=2, tiled=True)  20.3 us
    another operation x3, local copies, waits for them, and re-layouts, pair_join(): return jnp.stack([first_part, second_part], axis=stack_axis)  10.7 us
    all_to_all x1, starting transfers between devices, per_device(): lax.all_to_all(input_rows.astype(jnp.bfloat16).reshape(experts_axis, capa...  10.5 us
  transfers between devices with their start and end apart: 14, of which 4 were waited for; matrix products, arithmetic and copies ran while one was open for 25% of the time, Pallas kernels for 0%

profile of v1, /device:TPU:1, one launch (start us, length us, event | category | flops | bytes accessed | tf_op | source)
XLA Modules:
  0.0 312.1 jit_solution(4653211412755513477)
XLA Ops:
  0.7 8.9 %collective-permute-start.2 = (bf16[512,448]{0,1:T(8,128)(2,1)}, bf16[512,448]{0,1:T(8,128)(2,1)S(1)}, u32[]{:S(2)}, u32[]{:S(2)}) collective-permute-start(bf16[512,448]{0,1:T(8,128)(2,1)} %bitcast.173), channel_id=1, source_target_pairs={{0,8},{8,0},{16,24},{24,16},{32,40},{40,32},{48,56},{56,48},{64,72... | collective-permute-start | bytes 1376264 | tf_op jit(solution)/shard_map/ppermute | solution.py:14
  15.9 8.1 %all-to-all-start.2 = ((bf16[64,2,448]{2,1,0:T(2,128)(2,1)}), bf16[64,2,448]{2,1,0:T(2,128)(2,1)S(1)}, u32[]{:S(2)}, u32[]{:S(2)}) async-start(bf16[64,2,448]{2,1,0:T(2,128)(2,1)} %select_convert_fusion.3), calls=%async_computation.2 | async-start | bytes 262144 | tf_op jit(solution)/shard_map/all_to_all | solution.py:63
  30.4 4.0 %all-to-all-done.2 = bf16[64,2,448]{2,1,0:T(2,128)(2,1)S(1)} async-done(((bf16[64,2,448]{2,1,0:T(2,128)(2,1)}), bf16[64,2,448]{2,1,0:T(2,128)(2,1)S(1)}, u32[]{:S(2)}, u32[]{:S(2)}) %all-to-all-start.2) | async-done | bytes 114720 | tf_op jit(solution)/shard_map/all_to_all | solution.py:63
  34.4 6.3 %all-to-all-start = ((bf16[64,2,448]{2,1,0:T(2,128)(2,1)}), bf16[64,2,448]{2,1,0:T(2,128)(2,1)S(1)}, u32[]{:S(2)}, u32[]{:S(2)}) async-start(bf16[64,2,448]{2,1,0:T(2,128)(2,1)} %broadcast_select_fusion), calls=%async_computation | async-start | bytes 262144 | tf_op jit(solution)/shard_map/all_to_all | solution.py:56
  41.6 9.5 %all-to-all-done = bf16[64,2,448]{2,1,0:T(2,128)(2,1)S(1)} async-done(((bf16[64,2,448]{2,1,0:T(2,128)(2,1)}), bf16[64,2,448]{2,1,0:T(2,128)(2,1)S(1)}, u32[]{:S(2)}, u32[]{:S(2)}) %all-to-all-start) | async-done | bytes 114720 | tf_op jit(solution)/shard_map/all_to_all | solution.py:56
  51.3 24.1 %all_gather.14 = bf16[128,3584]{0,1:T(8,128)(2,1)} all-gather(bf16[128,448]{0,1:T(8,128)(2,1)S(1)} %copy.66), channel_id=1, replica_groups=mesh['expert'=64,'replica'=8] {'replica'}, dimensions={1}, use_global_device_ids=true | all-gather | bytes 1032192 | tf_op jit(solution)/shard_map/all_gather | solution.py:115
  77.7 6.0 %all-to-all-start.3 = ((bf16[2,512,448]{2,0,1:T(2,128)(2,1)}), bf16[2,512,448]{2,0,1:T(2,128)(2,1)}, u32[]{:S(2)}, u32[]{:S(2)}) async-start(bf16[2,512,448]{2,0,1:T(2,128)(2,1)} %copy.67), calls=%async_computation.3 | async-start | bytes 2097152 | tf_op jit(solution)/shard_map/all_to_all | solution.py:116
  83.7 41.3 %all_gather.12 = bf16[128,3584]{0,1:T(8,128)(2,1)S(1)} all-gather(bf16[128,448]{0,1:T(8,128)(2,1)S(1)} %copy.61), channel_id=1, replica_groups=mesh['expert'=64,'replica'=8] {'replica'}, dimensions={1}, use_global_device_ids=true | all-gather | bytes 1032192 | tf_op jit(solution)/shard_map/all_gather | solution.py:80
  128.1 4.3 %copy.75 = bf16[2,64,3584]{1,0,2:T(2,128)(2,1)S(1)} copy(bf16[2,64,3584]{2,1,0:T(8,128)(2,1)} %pad_maximum_fusion.2) | data formatting | bytes 1835008 | tf_op jit(solution)/shard_map/stack | solution.py:20
  134.5 4.2 %all-to-all-start.6 = ((bf16[8,2,28672]{2,1,0:T(2,128)(2,1)}), bf16[8,2,28672]{2,1,0:T(2,128)(2,1)}, u32[]{:S(2)}, u32[]{:S(2)}) async-start(bf16[8,2,28672]{2,1,0:T(2,128)(2,1)} %reshape.373), calls=%async_computation.6 | async-start | bytes 1835008 | tf_op jit(solution)/shard_map/all_to_all | solution.py:133
  141.9 4.3 %copy.71 = bf16[2,64,3584]{1,0,2:T(2,128)(2,1)S(1)} copy(bf16[2,64,3584]{2,1,0:T(8,128)(2,1)} %pad_maximum_fusion.1) | data formatting | bytes 1835008 | tf_op jit(solution)/shard_map/stack | solution.py:20
  156.8 6.5 %all-to-all-start.5 = ((bf16[8,2,28672]{2,1,0:T(2,128)(2,1)}), bf16[8,2,28672]{2,1,0:T(2,128)(2,1)}, u32[]{:S(2)}, u32[]{:S(2)}) async-start(bf16[8,2,28672]{2,1,0:T(2,128)(2,1)} %reshape.375), calls=%async_computation.5 | async-start | bytes 1835008 | tf_op jit(solution)/shard_map/all_to_all | solution.py:132
  164.2 31.6 %all_gather.13 = bf16[128,2,512]{0,2,1:T(8,128)(2,1)S(1)} all-gather(bf16[128,2,64]{0,2,1:T(8,128)(2,1)S(1)} %get-tuple-element.61), channel_id=1, replica_groups=mesh['expert'=64,'replica'=8] {'replica'}, dimensions={2}, use_global_device_ids=true | all-gather | bytes 294912 | tf_op jit(solution)/shard_map/all_gather | solution.py:98
  198.8 5.3 %reshape.374 = bf16[3584,2,64]{2,1,0:T(2,128)(2,1)} reshape(bf16[8,2,28672]{2,1,0:T(2,128)(2,1)} %all-to-all-done.6) | data formatting | bytes 1835008
  204.1 5.9 %copy.76 = bf16[2,64,8,448]{3,1,2,0:T(8,128)(2,1)} copy(bf16[2,64,8,448]{1,0,3,2:T(2,128)(2,1)} %bitcast.167) | data formatting | bytes 1835008 | tf_op jit(solution)/shard_map/all_to_all | solution.py:133
  209.9 13.0 %collective-permute-start.3 = (bf16[64,3584]{1,0:T(8,128)(2,1)}, bf16[64,3584]{1,0:T(8,128)(2,1)}, u32[]{:S(2)}, u32[]{:S(2)}) collective-permute-start(bf16[64,3584]{1,0:T(8,128)(2,1)} %select_convert_fusion.2), channel_id=1, source_target_pairs={{0,8},{8,0},{16,24},{24,16},{32,40},{40,32},{48,56},{56,48},{64,72... | collective-permute-start | bytes 1376264 | tf_op jit(solution)/shard_map/ppermute | solution.py:14
  227.4 4.9 %all-to-all-start.1 = ((bf16[64,2,448]{2,1,0:T(2,128)(2,1)}), bf16[64,2,448]{2,1,0:T(2,128)(2,1)S(1)}, u32[]{:S(2)}, u32[]{:S(2)}) async-start(bf16[64,2,448]{2,1,0:T(2,128)(2,1)} %reshape.220), calls=%async_computation.1 | async-start | bytes 262144 | tf_op jit(solution)/shard_map/all_to_all | solution.py:103
  234.0 8.7 %all-to-all-done.1 = bf16[64,2,448]{2,1,0:T(2,128)(2,1)S(1)} async-done(((bf16[64,2,448]{2,1,0:T(2,128)(2,1)}), bf16[64,2,448]{2,1,0:T(2,128)(2,1)S(1)}, u32[]{:S(2)}, u32[]{:S(2)}) %all-to-all-start.1) | async-done | bytes 114720 | tf_op jit(solution)/shard_map/all_to_all | solution.py:103
  243.4 4.9 %all-to-all-start.4 = ((bf16[8,128,2,64]{1,3,2,0:T(8,128)(2,1)}), bf16[8,128,2,64]{1,3,2,0:T(8,128)(2,1)S(1)}, u32[]{:S(2)}, u32[]{:S(2)}) async-start(bf16[8,128,2,64]{1,3,2,0:T(8,128)(2,1)} %stack.47), calls=%async_computation.4 | async-start | bytes 524288 | tf_op jit(solution)/shard_map/all_to_all | solution.py:126
  253.2 20.3 %all_gather.15 = bf16[128,2,512]{0,2,1:T(8,128)(2,1)S(1)} all-gather(bf16[128,2,64]{0,2,1:T(8,128)(2,1)S(1)} %get-tuple-element.60), channel_id=1, replica_groups=mesh['expert'=64,'replica'=8] {'replica'}, dimensions={2}, use_global_device_ids=true | all-gather | bytes 294912 | tf_op jit(solution)/shard_map/all_gather | solution.py:129
  274.1 5.3 %reshape.376 = bf16[3584,2,64]{2,1,0:T(2,128)(2,1)} reshape(bf16[8,2,28672]{2,1,0:T(2,128)(2,1)} %all-to-all-done.5) | data formatting | bytes 1835008
  279.4 4.6 %copy.72 = bf16[2,64,8,448]{3,1,2,0:T(8,128)(2,1)S(1)} copy(bf16[2,64,8,448]{1,0,3,2:T(2,128)(2,1)} %bitcast.168) | data formatting | bytes 1835008 | tf_op jit(solution)/shard_map/all_to_all | solution.py:132
  289.6 10.5 %all-to-all-start.7 = ((bf16[64,2,448]{2,1,0:T(2,128)(2,1)}), bf16[64,2,448]{2,1,0:T(2,128)(2,1)S(1)}, u32[]{:S(2)}, u32[]{:S(2)}) async-start(bf16[64,2,448]{2,1,0:T(2,128)(2,1)} %reshape.226), calls=%async_computation.7 | async-start | bytes 262144 | tf_op jit(solution)/shard_map/all_to_all | solution.py:141
  306.3 4.2 %all-to-all-done.7 = bf16[64,2,448]{2,1,0:T(2,128)(2,1)S(1)} async-done(((bf16[64,2,448]{2,1,0:T(2,128)(2,1)}), bf16[64,2,448]{2,1,0:T(2,128)(2,1)S(1)}, u32[]{:S(2)}, u32[]{:S(2)}) %all-to-all-start.7) | async-done | bytes 114720 | tf_op jit(solution)/shard_map/all_to_all | solution.py:141
  (123 shorter events, 64.2 us)
Async XLA Ops:
  0.6 10.5 %copy-start = (bf16[12,448]{1,0:T(8,128)(2,1)S(1)}, bf16[12,448]{1,0:T(8,128)(2,1)}, u32[]{:S(2)}) copy-start(bf16[12,448]{1,0:T(8,128)(2,1)} %param.21) | copy-start | bytes 32260
  0.6 27.7 %copy-start.19 = (s32[12,8]{0,1:T(8,128)S(1)}, s32[12,8]{0,1:T(8,128)}, u32[]{:S(2)}) copy-start(s32[12,8]{0,1:T(8,128)} %param.16) | copy-start | bytes 1156
  0.7 27.7 %copy-start.1 = (bf16[12,448]{1,0:T(8,128)(2,1)S(1)}, bf16[12,448]{1,0:T(8,128)(2,1)}, u32[]{:S(2)}) copy-start(bf16[12,448]{1,0:T(8,128)(2,1)} %param.15) | copy-start | bytes 32260
  0.7 74.7 %collective-permute-start.2 = (bf16[512,448]{0,1:T(8,128)(2,1)}, bf16[512,448]{0,1:T(8,128)(2,1)S(1)}, u32[]{:S(2)}, u32[]{:S(2)}) collective-permute-start(bf16[512,448]{0,1:T(8,128)(2,1)} %bitcast.173), channel_id=1, source_target_pairs={{0,8},{8,0},{16,24},{24,16},{32,40},{40,32},{48,56},{56,48},{64,72... | collective-permute-start | bytes 1376264 | tf_op jit(solution)/shard_map/ppermute | solution.py:14
  15.9 18.4 %all-to-all-start.2 = ((bf16[64,2,448]{2,1,0:T(2,128)(2,1)}), bf16[64,2,448]{2,1,0:T(2,128)(2,1)S(1)}, u32[]{:S(2)}, u32[]{:S(2)}) async-start(bf16[64,2,448]{2,1,0:T(2,128)(2,1)} %select_convert_fusion.3), calls=%async_computation.2 | async-start | bytes 262144 | tf_op jit(solution)/shard_map/all_to_all | solution.py:63
  24.0 101.0 %collective-permute-start.1 = (bf16[64,3584]{1,0:T(8,128)(2,1)}, bf16[64,3584]{1,0:T(8,128)(2,1)}, u32[]{:S(2)}, u32[]{:S(2)}) collective-permute-start(bf16[64,3584]{1,0:T(8,128)(2,1)} %bitcast.6), channel_id=1, source_target_pairs={{0,8},{8,0},{16,24},{24,16},{32,40},{40,32},{48,56},{56,48},{64,72... | collective-permute-start | bytes 1376264 | tf_op jit(solution)/shard_map/ppermute | solution.py:14
  26.4 112.4 %collective-permute-start = (bf16[64,3584]{1,0:T(8,128)(2,1)}, bf16[64,3584]{1,0:T(8,128)(2,1)}, u32[]{:S(2)}, u32[]{:S(2)}) collective-permute-start(bf16[64,3584]{1,0:T(8,128)(2,1)} %bitcast.3), channel_id=1, source_target_pairs={{0,8},{8,0},{16,24},{24,16},{32,40},{40,32},{48,56},{56,48},{64,72... | collective-permute-start | bytes 1376264 | tf_op jit(solution)/shard_map/ppermute | solution.py:14
  28.4 47.0 %copy-start.16 = (bf16[1,512,448]{1,2,0:T(8,128)(2,1)S(1)}, bf16[1,512,448]{1,2,0:T(8,128)(2,1)}, u32[]{:S(2)}) copy-start(bf16[1,512,448]{1,2,0:T(8,128)(2,1)} %param.20) | copy-start | bytes 1376260
  34.4 16.7 %all-to-all-start = ((bf16[64,2,448]{2,1,0:T(2,128)(2,1)}), bf16[64,2,448]{2,1,0:T(2,128)(2,1)S(1)}, u32[]{:S(2)}, u32[]{:S(2)}) async-start(bf16[64,2,448]{2,1,0:T(2,128)(2,1)} %broadcast_select_fusion), calls=%async_computation | async-start | bytes 262144 | tf_op jit(solution)/shard_map/all_to_all | solution.py:56
  75.5 2.2 copy-start.6
  77.7 56.9 %all-to-all-start.3 = ((bf16[2,512,448]{2,0,1:T(2,128)(2,1)}), bf16[2,512,448]{2,0,1:T(2,128)(2,1)}, u32[]{:S(2)}, u32[]{:S(2)}) async-start(bf16[2,512,448]{2,0,1:T(2,128)(2,1)} %copy.67), calls=%async_computation.3 | async-start | bytes 2097152 | tf_op jit(solution)/shard_map/all_to_all | solution.py:116
  134.5 22.2 %all-to-all-start.6 = ((bf16[8,2,28672]{2,1,0:T(2,128)(2,1)}), bf16[8,2,28672]{2,1,0:T(2,128)(2,1)}, u32[]{:S(2)}, u32[]{:S(2)}) async-start(bf16[8,2,28672]{2,1,0:T(2,128)(2,1)} %reshape.373), calls=%async_computation.6 | async-start | bytes 1835008 | tf_op jit(solution)/shard_map/all_to_all | solution.py:133
  151.9 4.0 %copy-start.10 = (bf16[1,64,3584]{2,1,0:T(8,128)(2,1)S(1)}, bf16[1,64,3584]{2,1,0:T(8,128)(2,1)}, u32[]{:S(2)}) copy-start(bf16[1,64,3584]{2,1,0:T(8,128)(2,1)} %copy-done.9) | copy-start | bytes 1376260
  156.8 70.6 %all-to-all-start.5 = ((bf16[8,2,28672]{2,1,0:T(2,128)(2,1)}), bf16[8,2,28672]{2,1,0:T(2,128)(2,1)}, u32[]{:S(2)}, u32[]{:S(2)}) async-start(bf16[8,2,28672]{2,1,0:T(2,128)(2,1)} %reshape.375), calls=%async_computation.5 | async-start | bytes 1835008 | tf_op jit(solution)/shard_map/all_to_all | solution.py:132
  209.9 90.2 %collective-permute-start.3 = (bf16[64,3584]{1,0:T(8,128)(2,1)}, bf16[64,3584]{1,0:T(8,128)(2,1)}, u32[]{:S(2)}, u32[]{:S(2)}) collective-permute-start(bf16[64,3584]{1,0:T(8,128)(2,1)} %select_convert_fusion.2), channel_id=1, source_target_pairs={{0,8},{8,0},{16,24},{24,16},{32,40},{40,32},{48,56},{56,48},{64,72... | collective-permute-start | bytes 1376264 | tf_op jit(solution)/shard_map/ppermute | solution.py:14
  222.9 9.4 %copy-start.14 = (bf16[128,2,512]{0,2,1:T(8,128)(2,1)S(1)}, bf16[128,2,512]{0,2,1:T(8,128)(2,1)}, u32[]{:S(2)}) copy-start(bf16[128,2,512]{0,2,1:T(8,128)(2,1)} %copy-done.13) | copy-start | bytes 786436
  225.5 76.7 %collective-permute-start.4 = (bf16[64,3584]{1,0:T(8,128)(2,1)}, bf16[64,3584]{1,0:T(8,128)(2,1)}, u32[]{:S(2)}, u32[]{:S(2)}) collective-permute-start(bf16[64,3584]{1,0:T(8,128)(2,1)} %select_convert_fusion.1), channel_id=1, source_target_pairs={{0,8},{8,0},{16,24},{24,16},{32,40},{40,32},{48,56},{56,48},{64,72... | collective-permute-start | bytes 1376264 | tf_op jit(solution)/shard_map/ppermute | solution.py:14
  227.4 15.3 %all-to-all-start.1 = ((bf16[64,2,448]{2,1,0:T(2,128)(2,1)}), bf16[64,2,448]{2,1,0:T(2,128)(2,1)S(1)}, u32[]{:S(2)}, u32[]{:S(2)}) async-start(bf16[64,2,448]{2,1,0:T(2,128)(2,1)} %reshape.220), calls=%async_computation.1 | async-start | bytes 262144 | tf_op jit(solution)/shard_map/all_to_all | solution.py:103
  232.3 41.3 %copy-start.5 = (bf16[2,64,8,448]{3,1,2,0:T(8,128)(2,1)S(1)}, bf16[2,64,8,448]{3,1,2,0:T(8,128)(2,1)}, u32[]{:S(2)}) copy-start(bf16[2,64,8,448]{3,1,2,0:T(8,128)(2,1)} %copy.76) | copy-start | bytes 2752516
  242.7 30.9 %copy-start.15 = (bf16[64,2,448]{2,1,0:T(2,128)(2,1)}, bf16[64,2,448]{2,1,0:T(2,128)(2,1)S(1)}, u32[]{:S(2)}) copy-start(bf16[64,2,448]{2,1,0:T(2,128)(2,1)S(1)} %all-to-all-done.1) | copy-start | bytes 344068
  243.4 44.8 %all-to-all-start.4 = ((bf16[8,128,2,64]{1,3,2,0:T(8,128)(2,1)}), bf16[8,128,2,64]{1,3,2,0:T(8,128)(2,1)S(1)}, u32[]{:S(2)}, u32[]{:S(2)}) async-start(bf16[8,128,2,64]{1,3,2,0:T(8,128)(2,1)} %stack.47), calls=%async_computation.4 | async-start | bytes 524288 | tf_op jit(solution)/shard_map/all_to_all | solution.py:126
  250.6 53.6 %collective-permute-start.5 = (bf16[512,448]{0,1:T(8,128)(2,1)}, bf16[512,448]{0,1:T(8,128)(2,1)}, u32[]{:S(2)}, u32[]{:S(2)}) collective-permute-start(bf16[512,448]{0,1:T(8,128)(2,1)} %select_convert_fusion), channel_id=1, source_target_pairs={{0,8},{8,0},{16,24},{24,16},{32,40},{40,32},{48,56},{56,48},{64,72... | collective-permute-start | bytes 1376264 | tf_op jit(solution)/shard_map/ppermute | solution.py:14
  279.4 7.2 %copy-start.18 = (f32[12,8]{1,0:T(8,128)S(1)}, f32[12,8]{1,0:T(8,128)}, u32[]{:S(2)}) copy-start(f32[12,8]{1,0:T(8,128)} %copy-done.17) | copy-start | bytes 1156
  289.6 20.9 %all-to-all-start.7 = ((bf16[64,2,448]{2,1,0:T(2,128)(2,1)}), bf16[64,2,448]{2,1,0:T(2,128)(2,1)S(1)}, u32[]{:S(2)}, u32[]{:S(2)}) async-start(bf16[64,2,448]{2,1,0:T(2,128)(2,1)} %reshape.226), calls=%async_computation.7 | async-start | bytes 262144 | tf_op jit(solution)/shard_map/all_to_all | solution.py:141
  (10 other events, 12.0 us)
